TPU v7x, 32 devices: a whole 2x2x4 slice. The times are simulated.
32 devices in a mesh: dp: 16 (over z, x, core), tensor: 2 (over y).
Axes of the slice: x: 2, y: 2, z: 4, core: 2. Of those that a mesh axis runs over, the one named last changes fastest.
Arguments:
- tokens: bfloat16 [16, 256, 8192], P('dp', None, 'tensor'), may hold values from -6 to 6
- segment_ids: int32 [16, 256], P('dp'), may hold values from 0 to 3, never falling along the last dimension, each value on 1 to 128 neighbouring positions
- queries: bfloat16 [16, 256, 8192], P('dp', None, 'tensor'), may hold values from -7 to 7
- teacher_keys: bfloat16 [16, 256, 1024], P('dp', None, 'tensor'), may hold values from -7 to 7
- teacher_values: bfloat16 [16, 256, 1024], P('dp', None, 'tensor'), may hold values from -6 to 6
- down_weight: bfloat16 [8192, 512], P('tensor'), may hold values from -0.0625 to 0.0625
- rope_weight: bfloat16 [64, 8192], P(None, 'tensor'), may hold values from -1 to 1
- key_up: bfloat16 [512, 4096], P(None, 'tensor'), may hold values from -0.25 to 0.25
- value_up: bfloat16 [512, 8192], P(None, 'tensor'), may hold values from -0.25 to 0.25
Outputs:
- grad_down: float32 [8192, 512], P('tensor')
- grad_rope: float32 [64, 8192], P(None, 'tensor')
- grad_key_up: float32 [512, 4096], P(None, 'tensor')
- grad_value_up: float32 [512, 8192], P(None, 'tensor')
Inputs may be any that keep to these rules, and one draw needn't show every extreme that they name: `segment_ids`: along a sequence the document number never falls; each of the 4 documents holds 1 to 128 tokens, and one holds exactly 128.
All inputs are finite; a program needn't handle non-finite values.
Results may differ from a plain program's by a relative error of at most 0.011.
Values sent between devices are 32-bit elements; how exact they have to be, the bound alone decides.
A program may use at most 128 MiB of HBM per device.

v0:
```python
import math

import jax
import jax.numpy as jnp
from jax import lax
from jax.sharding import PartitionSpec as P

HEAD = 128
ROPE = 64


theta_base = 500000.0
norm_eps = 1e-06


def angle_tables(positions, width):
    half_width = width // 2
    exponent = jnp.arange(half_width, dtype=jnp.float32) * (2.0 / width)
    frequency = jnp.exp(-exponent * jnp.log(jnp.float32(theta_base)))
    angles = positions.astype(jnp.float32)[:, None] * frequency[None, :]
    return (jnp.cos(angles), jnp.sin(angles))


def rotate_last(tensor, cosine, sine_tab):
    half_width = tensor.shape[-1] // 2
    first_half = tensor[..., :half_width]
    second_half = tensor[..., half_width:]
    return jnp.concatenate(
        [
            first_half * cosine - second_half * sine_tab,
            second_half * cosine + first_half * sine_tab,
        ],
        axis=-1,
    )


def rotate_rows(matrix, cosine, sine_tab):
    half_width = matrix.shape[0] // 2
    first_half = matrix[:half_width]
    second_half = matrix[half_width:]
    return jnp.concatenate(
        [
            first_half * cosine - second_half * sine_tab,
            second_half * cosine + first_half * sine_tab,
        ],
        axis=0,
    )


def unrotate_rows(matrix, cosine, sine_tab):
    half_width = matrix.shape[0] // 2
    first_half = matrix[:half_width]
    second_half = matrix[half_width:]
    return jnp.concatenate(
        [
            first_half * cosine + second_half * sine_tab,
            second_half * cosine - first_half * sine_tab,
        ],
        axis=0,
    )


def doc_positions(segments_row):
    position_index = jnp.arange(segments_row.shape[0], dtype=jnp.int32)
    is_start = jnp.concatenate(
        [jnp.ones((1,), dtype=jnp.bool_), segments_row[1:] != segments_row[:-1]]
    )
    doc_start = lax.cummax(jnp.where(is_start, position_index, 0), axis=0)
    return position_index - doc_start


def block_mask(seg_block, segments_row, row_start):
    rows_index = row_start + jnp.arange(seg_block.shape[0], dtype=jnp.int32)
    cols_index = jnp.arange(segments_row.shape[0], dtype=jnp.int32)
    return (
        (seg_block[:, None] == segments_row[None, :]) & (cols_index[None, :] <= rows_index[:, None])
    ).astype(jnp.int32)


def masked_softmax(scores, doc_mask):
    masked = jnp.where(doc_mask > 0, scores, -jnp.inf)
    peak = jnp.max(masked, axis=-1, keepdims=True)
    weights = jnp.exp(masked - peak)
    return weights / jnp.sum(weights, axis=-1, keepdims=True)


def local(
    tokens,
    segment_ids,
    queries,
    teacher_keys,
    teacher_values,
    down_weight,
    rope_weight,
    key_up,
    value_up,
):
    f32 = jnp.float32
    bf16 = jnp.bfloat16
    token_rows = tokens[0]
    segments_row = segment_ids[0]
    seq_len = token_rows.shape[0]
    heads_local = queries.shape[2] // HEAD
    kv_local = teacher_keys.shape[2] // HEAD
    group_size = heads_local // kv_local
    nope_width = HEAD - ROPE
    score_scale = 1.0 / math.sqrt(HEAD)
    contract_cols = (((1,), (1,)), ((), ()))
    contract_rows = (((0,), (0,)), ((), ()))
    positions = doc_positions(segments_row)
    cos_full, sin_full = angle_tables(positions, HEAD)
    cos_rope, sin_rope = angle_tables(positions, ROPE)
    latent_part = jnp.dot(token_rows, down_weight, preferred_element_type=f32)
    rope_part = lax.dot_general(rope_weight, token_rows, contract_cols, preferred_element_type=f32)
    latent_raw, rope_sum = lax.psum((latent_part, rope_part), "tensor")
    inv_rms = lax.rsqrt(jnp.mean(latent_raw * latent_raw, axis=-1, keepdims=True) + norm_eps)
    normed = latent_raw * inv_rms
    latent = normed.astype(bf16)
    rope_key = rotate_rows(rope_sum, cos_rope.T, sin_rope.T).astype(bf16)
    head_queries = queries[0].reshape(seq_len, heads_local, HEAD).transpose(1, 0, 2)
    teacher_q = (
        rotate_last(head_queries.astype(f32), cos_full, sin_full)
        .astype(bf16)
        .reshape(kv_local, group_size, seq_len, HEAD)
    )
    teacher_k = rotate_last(
        teacher_keys[0].reshape(seq_len, kv_local, HEAD).transpose(1, 0, 2).astype(f32),
        cos_full,
        sin_full,
    ).astype(bf16)
    teacher_v = teacher_values[0].reshape(seq_len, kv_local, HEAD).transpose(1, 0, 2)
    key_nope = (
        jnp.dot(latent, key_up, preferred_element_type=f32)
        .astype(bf16)
        .reshape(seq_len, heads_local, nope_width)
        .transpose(1, 0, 2)
    )
    head_values = (
        jnp.dot(latent, value_up, preferred_element_type=f32)
        .astype(bf16)
        .reshape(seq_len, heads_local, HEAD)
        .transpose(1, 0, 2)
    )
    rotated_q = rotate_last(head_queries[..., :ROPE].astype(f32), cos_rope, sin_rope).astype(bf16)
    student_q = jnp.concatenate([head_queries[..., ROPE:], rotated_q], axis=-1)
    student_k = jnp.concatenate(
        [key_nope, jnp.broadcast_to(rope_key.T[None], (heads_local, seq_len, ROPE))], axis=-1
    )
    block_rows = min(seq_len, 512)
    block_count = seq_len // block_rows

    def attend_block(carry, block_index):
        value_acc, key_acc = carry
        row_start = block_index * block_rows
        doc_mask = block_mask(segments_row, segments_row, row_start)
        teacher_scores = (
            jnp.einsum("kgqd,kpd->kgqp", teacher_q, teacher_k, preferred_element_type=f32)
            * score_scale
        )
        teacher_weights = masked_softmax(teacher_scores, doc_mask).astype(bf16)
        teacher_out = jnp.einsum(
            "kgqp,kpd->kgqd", teacher_weights, teacher_v, preferred_element_type=f32
        ).reshape(heads_local, block_rows, HEAD)
        student_scores = (
            jnp.einsum("hqd,hpd->hqp", student_q, student_k, preferred_element_type=f32)
            * score_scale
        )
        student_weights = masked_softmax(student_scores, doc_mask)
        student_low = student_weights.astype(bf16)
        student_out = jnp.einsum(
            "hqp,hpd->hqd", student_low, head_values, preferred_element_type=f32
        )
        out_grad = (student_out - teacher_out).astype(bf16)
        weight_grad = jnp.einsum("hqd,hpd->hqp", out_grad, head_values, preferred_element_type=f32)
        row_dot = jnp.sum(student_weights * weight_grad, axis=-1, keepdims=True)
        score_grad = (student_weights * (weight_grad - row_dot) * score_scale).astype(bf16)
        value_acc = value_acc + jnp.einsum(
            "hqp,hqd->hpd", student_low, out_grad, preferred_element_type=f32
        )
        key_acc = key_acc + jnp.einsum(
            "hqp,hqd->hpd", score_grad, student_q, preferred_element_type=f32
        )
        return ((value_acc, key_acc), None)

    zeros_acc = jnp.zeros((heads_local, seq_len, HEAD), f32)
    accums, unused = lax.scan(
        attend_block, (zeros_acc, zeros_acc), jnp.arange(block_count, dtype=jnp.int32)
    )
    value_acc, key_acc = accums
    value_flat = value_acc.astype(bf16).transpose(1, 0, 2).reshape(seq_len, heads_local * HEAD)
    nope_grad = (
        key_acc[..., :nope_width]
        .astype(bf16)
        .transpose(1, 0, 2)
        .reshape(seq_len, heads_local * nope_width)
    )
    rope_grad_part = jnp.sum(key_acc[..., nope_width:], axis=0).T
    norm_grad_part = lax.dot_general(
        nope_grad, key_up, contract_cols, preferred_element_type=f32
    ) + lax.dot_general(value_flat, value_up, contract_cols, preferred_element_type=f32)
    grad_kup = lax.dot_general(latent, nope_grad, contract_rows, preferred_element_type=f32)
    grad_vup = lax.dot_general(latent, value_flat, contract_rows, preferred_element_type=f32)
    norm_grad, rope_grad_sum = lax.psum((norm_grad_part, rope_grad_part), "tensor")
    latent_grad = (
        (norm_grad - normed * jnp.mean(norm_grad * normed, axis=-1, keepdims=True)) * inv_rms
    ).astype(bf16)
    rope_grad = unrotate_rows(rope_grad_sum, cos_rope.T, sin_rope.T).astype(bf16)
    grad_down = lax.dot_general(token_rows, latent_grad, contract_rows, preferred_element_type=f32)
    grad_rope = jnp.dot(rope_grad, token_rows, preferred_element_type=f32)
    grad_down, grad_rope, grad_kup, grad_vup = lax.psum(
        (grad_down, grad_rope, grad_kup, grad_vup), "dp"
    )
    return (grad_down, grad_rope, grad_kup, grad_vup)


def solution(mesh):
    in_specs = (
        P("dp", None, "tensor"),
        P("dp", None),
        P("dp", None, "tensor"),
        P("dp", None, "tensor"),
        P("dp", None, "tensor"),
        P("tensor", None),
        P(None, "tensor"),
        P(None, "tensor"),
        P(None, "tensor"),
    )
    out_specs = (P("tensor", None), P(None, "tensor"), P(None, "tensor"), P(None, "tensor"))
    return jax.shard_map(local, mesh=mesh, in_specs=in_specs, out_specs=out_specs, check_vma=False)
```

profile of v0, /device:TPU:0, one launch (start us, length us, event | category | flops | bytes accessed | tf_op | source)
XLA Modules:
  0.0 561.9 jit_solution(919850631514819260)
XLA Ops:
  7.2 0.0 all-reduce.11.cloned.1.call-start
  7.2 1.5 copy-done
  8.8 2.4 fusion.32
  11.2 4.3 fusion.34
  15.5 0.0 all-reduce.11.cloned.1.call-update
  15.5 0.0 all-reduce.9.cloned.1.call-start
  15.6 0.1 compare_reduce_fusion
  15.7 0.1 fusion.71
  15.8 0.3 reduce-window.9
  16.1 0.1 slice.63
  16.2 0.1 slice_reduce_fusion.1
  16.3 0.1 fusion.72
  16.4 0.1 convert_compare_fusion
  16.5 0.1 copy.31
  16.6 0.1 copy.32
  16.8 0.1 reshape_squeeze.8
  16.9 4.1 copy.24
  20.9 4.1 copy.25
  25.0 2.1 bitcast_convert_fusion
  27.1 0.5 multiply_cosine_fusion
  27.6 0.3 subtract_convert_fusion.2
  27.9 1.4 subtract_convert_fusion
  29.4 0.2 copy-done.1
  29.5 2.2 fusion.82
  31.7 1.6 fusion.25
  33.3 4.5 fusion.83
  37.8 7.3 %fusion.17 = f32[4,8,256,128]{3,2,1,0:T(8,128)} fusion(f32[4,8,256,256]{2,3,1,0:T(8,128)} %get-tuple-element.67, f32[4,8,256]{2,1,0:T(8,128)S(1)} %get-tuple-element.66, bf16[256,4,128]{2,1,0:T(4,128)(2,1)S(1)} %reshape_squeeze.8), kind=kOutput, calls=%fused_computation.28 | convolution fusion | flops 541065216 | bytes 12877824 | tf_op jit(solution)/shard_map/while/body/eval_jaxpr/kgqp,kpd->kgqd/dot_general | solution.py:161
  45.1 0.5 multiply_cosine_fusion.1
  45.6 3.5 subtract_convert_fusion.1
  49.1 1.0 fusion.61
  50.1 1.2 multiply_reduce_fusion.2
  51.3 0.1 copy.28
  51.4 1.1 multiply_convert_fusion.2
  52.5 3.3 convolution_convert_fusion.1
  55.8 1.5 copy.26
  57.3 1.8 copy.27
  59.1 4.9 fusion.44
  64.0 0.5 broadcast_in_dim.33
  64.5 3.3 fusion.21
  67.8 4.6 fusion.84
  72.4 6.4 %fusion.11 = bf16[32,256,128]{2,1,0:T(8,128)(2,1)S(1)} fusion(f32[4,8,256,128]{3,2,1,0:T(8,128)} %fusion.17, bf16[32,32,8,128]{3,2,1,0:T(8,128)(2,1)S(1)} %copy-done.11, f32[32,256,256]{1,2,0:T(8,128)} %get-tuple-element.69, f32[32,256]{1,0:T(8,128)S(1)} %get-tuple-element.68), kind=kOutput, calls=%fused_computation.17 | convolution fusion | flops 543162368 | bytes 16809984 | tf_op jit(solution)/shard_map/while/body/eval_jaxpr/hqp,hpd->hqd/dot_general | solution.py:170
  78.8 0.6 copy-done.16
  79.4 2.9 fusion.39
  82.2 4.7 fusion.20
  86.9 16.9 %fusion.9 = f32[32,256,128]{1,2,0:T(8,128)} fusion(f32[32,256,256]{1,2,0:T(8,128)} %fusion.20, bf16[32,256,32]{2,1,0:T(8,128)(2,1)} %get-tuple-element.51, bf16[32,256,32]{2,1,0:T(8,128)(2,1)} %get-tuple-element.50, bf16[32,256,64]{2,1,0:T(8,128)(2,1)} %get-tuple-element.54, f32[32,256,256]{1,2,0:T(8,128)} %get-tuple-element.69, ...), kind=kOutput, calls=%fused_computation.15 | convolution fusion | flops 557850880 | bytes 23101440 | tf_op jit(solution)/shard_map/while/body/eval_jaxpr/hqp,hqd->hpd/dot_general | solution.py:180
  103.8 2.5 slice_reduce_fusion
  106.3 1.7 slice.116
  108.1 3.7 fusion.85
  111.8 1.6 convolution_add_fusion
  113.3 0.0 all-reduce.9.cloned.1.call-update
  113.4 0.0 all-reduce.7.cloned.1.call-start
  113.4 2.8 fusion.86
  116.2 4.7 fusion.87
  120.9 25.5 %all-reduce.9.cloned.1.call-done = (f32[256,512]{1,0:T(8,128)}, f32[64,256]{1,0:T(8,128)}) async-done(((f32[256,512]{1,0:T(8,128)}, f32[64,256]{1,0:T(8,128)}), (f32[256,512]{1,0:T(8,128)}, f32[64,256]{1,0:T(8,128)})) %all-reduce.9.cloned.1.call-update) | async-done | bytes 589840 | tf_op jit(solution)/shard_map/psum | solution.py:203
  146.4 1.0 fusion.65
  147.4 1.2 multiply_reduce_fusion.1
  148.6 5.9 %convolution_bitcast_fusion = f32[4096,512]{0,1:T(8,128)} fusion(bf16[1,256,4096]{2,1,0:T(8,128)(2,1)S(1)} %copy-done, f32[256,512]{1,0:T(8,128)} %get-tuple-element.46, f32[256,512]{1,0:T(8,128)S(1)} %copy-done.6, f32[256]{0:T(256)S(1)} %broadcast_multiply_fusion, f32[256]{0:T(256)S(1)} %add_rsqrt_fusion), kind=kOutput, calls=%fused_computation.11 | convolution fusion | flops 1074397184 | bytes 11536384 | tf_op jit(solution)/shard_map/dot_general | solution.py:208
  154.5 1.5 fusion.29
  156.0 379.9 %all-reduce.7.cloned.1.call-done = (f32[4096,512]{0,1:T(8,128)}, f32[64,4096]{1,0:T(8,128)}, f32[512,2048]{1,0:T(8,128)}, f32[512,4096]{1,0:T(8,128)}) async-done(((f32[4096,512]{0,1:T(8,128)}, f32[64,4096]{1,0:T(8,128)}, f32[512,2048]{1,0:T(8,128)}, f32[512,4096]{1,0:T(8,128)}), (f32[4096,512]{0,1:T(8,128)}, f32[64,4096]{1,0:T(8,128)}, f32[512,2048]{1,0:T(8,128)}, ...) | async-done | bytes 22020112 | tf_op jit(solution)/shard_map/psum | solution.py:210
  535.8 9.0 %copy.39 = f32[4096,512]{1,0:T(8,128)} copy(f32[4096,512]{0,1:T(8,128)} %get-tuple-element.42) | data formatting | bytes 16777216
  544.9 1.0 copy.69
  545.8 5.0 copy.70
  550.8 1.2 copy-done.7
  552.0 3.4 copy.71
  (38 shorter events, 0.2 us)
Async XLA Ops:
  7.2 1.6 copy-start
  7.2 41.9 %all-reduce.11.cloned.1.call-start = ((), (), s32[]{:S(2)}) async-start(), calls=%async_computation.2 | async-start | bytes 1179648 | tf_op jit(solution)/shard_map/psum | solution.py:115
  11.2 4.4 copy-start.15
  11.2 5.3 copy-start.13
  11.2 5.6 copy-start.14
  15.5 130.9 %all-reduce.9.cloned.1.call-start = ((), (), s32[]{:S(2)}) async-start(), calls=%async_computation.1 | async-start | bytes 1179648 | tf_op jit(solution)/shard_map/psum | solution.py:203
  27.9 1.6 copy-start.1
  59.1 5.4 copy-start.2
  59.1 5.4 copy-start.3
  59.1 5.4 copy-start.4
  59.1 5.4 copy-start.5
  67.8 4.6 copy-start.11
  72.4 7.0 %copy-start.16 = (f32[32,256,256]{1,2,0:T(8,128)S(1)}, f32[32,256,256]{1,2,0:T(8,128)}, u32[]{:S(2)}) copy-start(f32[32,256,256]{1,2,0:T(8,128)} %get-tuple-element.69) | copy-start | bytes 25165828
  103.8 4.3 copy-start.9
  108.1 3.7 copy-start.8
  113.4 422.5 %all-reduce.7.cloned.1.call-start = ((), (), s32[]{:S(2)}) async-start(), calls=%async_computation | async-start | bytes 44040192 | tf_op jit(solution)/shard_map/psum | solution.py:210
  113.4 2.8 copy-start.10
  116.2 31.2 %copy-start.6 = (f32[256,512]{1,0:T(8,128)S(1)}, f32[256,512]{1,0:T(8,128)}, u32[]{:S(2)}) copy-start(f32[256,512]{1,0:T(8,128)} %get-tuple-element.48) | copy-start | bytes 1572868
  535.8 9.0 %copy-start.12 = (f32[64,4096]{1,0:T(8,128)S(1)}, f32[64,4096]{1,0:T(8,128)}, u32[]{:S(2)}) copy-start(f32[64,4096]{1,0:T(8,128)} %get-tuple-element.71) | copy-start | bytes 3145732
  545.8 6.2 %copy-start.7 = (f32[512,4096]{1,0:T(8,128)S(1)}, f32[512,4096]{1,0:T(8,128)}, u32[]{:S(2)}) copy-start(f32[512,4096]{1,0:T(8,128)} %get-tuple-element.73) | copy-start | bytes 25165828
Sparse Core Ops, SparseCore 0:
  15.6 32.9 all-reduce.10
  113.5 32.8 all-reduce.8
  156.1 379.7 all-reduce.6
where the time goes:
time: 563 us; the launch traced here: 562 us
  waiting for transfers between devices  405 us (72%)
  matrix products  77.9 us (14%)
  local copies, waits for them, and re-layouts  36.1 us (6%)
  other arithmetic  28.3 us (5%)
  between operations  14 us (2%)
    psum x1, waiting for transfers between devices, local(): lax.psum((grad_down, grad_rope, grad_kup, grad_vup), 'dp')  380 us
    unnamed x40, local copies, waits for them, and re-layouts  26.1 us
    psum x1, waiting for transfers between devices, local(): lax.psum((norm_grad_part, rope_grad_part), 'tensor')  25.5 us
    dot_general x1, matrix products, attend_block(): jnp.einsum('hqp,hqd->hpd', score_grad, student_q, preferred_element_type=...  16.9 us
  transfers between devices with their start and end apart: 3, of which 2 were waited for; matrix products, arithmetic and copies ran while one was open for 7% of the time, Pallas kernels for 0%

commit v1 on v0

--- a/solution.py
+++ b/solution.py
@@ -62,11 +62,8 @@
 
 def doc_positions(segments_row):
     position_index = jnp.arange(segments_row.shape[0], dtype=jnp.int32)
-    is_start = jnp.concatenate(
-        [jnp.ones((1,), dtype=jnp.bool_), segments_row[1:] != segments_row[:-1]]
-    )
-    doc_start = lax.cummax(jnp.where(is_start, position_index, 0), axis=0)
-    return position_index - doc_start
+    earlier = (segments_row[None, :] < segments_row[:, None]).astype(jnp.int32)
+    return position_index - jnp.sum(earlier, axis=1)
 
 
 def block_mask(seg_block, segments_row, row_start):

time: 563 us -> 562 us (level)
  transfers between devices with their start and end apart: 3 -> 3, of which waited for: 2 -> 3; matrix products, arithmetic and copies ran while one was open for 7% -> 7% of each run, Pallas kernels for 0% -> 0%
where the time goes in v1:
time: 562 us; the launch traced here: 561 us
  waiting for transfers between devices  406 us (72%)
  matrix products  77.8 us (14%)
  local copies, waits for them, and re-layouts  35.9 us (6%)
  other arithmetic  27.9 us (5%)
  between operations  14.1 us (3%)
    psum x1, waiting for transfers between devices, local(): lax.psum((grad_down, grad_rope, grad_kup, grad_vup), 'dp')  380 us
    unnamed x40, local copies, waits for them, and re-layouts  26.1 us
    psum x1, waiting for transfers between devices, local(): lax.psum((norm_grad_part, rope_grad_part), 'tensor')  25.4 us
    dot_general x1, matrix products, attend_block(): jnp.einsum('hqp,hqd->hpd', score_grad, student_q, preferred_element_type=...  16.8 us
  transfers between devices with their start and end apart: 3, of which 3 were waited for; matrix products, arithmetic and copies ran while one was open for 7% of the time, Pallas kernels for 0%

profile of v1, /device:TPU:0, one launch (start us, length us, event | category | flops | bytes accessed | tf_op | source)
XLA Modules:
  0.0 561.2 jit_solution(14315382197918661275)
XLA Ops:
  7.2 0.0 copy-start
  7.2 0.0 all-reduce.11.cloned.1.call-start
  7.2 1.5 copy-done
  8.8 2.4 fusion.32
  11.2 4.3 fusion.34
  15.5 0.0 all-reduce.11.cloned.1.call-update
  15.5 0.0 all-reduce.9.cloned.1.call-start
  15.6 0.1 convert_reduce_fusion
  15.7 0.1 convert_compare_fusion
  15.8 0.1 copy.31
  16.0 0.1 copy.32
  16.1 0.1 reshape_squeeze.8
  16.2 4.1 copy.24
  20.3 4.1 copy.25
  24.3 2.1 bitcast_convert_fusion
  26.4 0.5 multiply_cosine_fusion
  27.0 0.3 subtract_convert_fusion.2
  27.2 0.0 copy-start.1
  27.3 1.4 subtract_convert_fusion
  28.7 0.1 copy-done.1
  28.8 2.2 fusion.80
  31.0 1.6 fusion.25
  32.6 4.5 fusion.81
  37.1 7.2 %fusion.17 = f32[4,8,256,128]{3,2,1,0:T(8,128)} fusion(f32[4,8,256,256]{2,3,1,0:T(8,128)} %get-tuple-element.67, f32[4,8,256]{2,1,0:T(8,128)S(1)} %get-tuple-element.66, bf16[256,4,128]{2,1,0:T(4,128)(2,1)S(1)} %reshape_squeeze.8), kind=kOutput, calls=%fused_computation.28 | convolution fusion | flops 541065216 | bytes 12877824 | tf_op jit(solution)/shard_map/while/body/eval_jaxpr/kgqp,kpd->kgqd/dot_general | solution.py:158
  44.4 0.5 multiply_cosine_fusion.1
  44.9 3.5 subtract_convert_fusion.1
  48.4 0.2 all-reduce.11.cloned.1.call-done
  48.6 1.0 fusion.61
  49.6 1.2 multiply_reduce_fusion.2
  50.7 0.1 copy.28
  50.9 1.1 multiply_convert_fusion.2
  52.0 3.3 convolution_convert_fusion.1
  55.3 1.5 copy.26
  56.8 1.8 copy.27
  58.6 4.9 fusion.44
  63.5 0.5 broadcast_in_dim.28
  64.0 3.3 fusion.21
  67.3 0.0 copy-start.11
  67.3 4.6 fusion.82
  71.9 6.4 %fusion.11 = bf16[32,256,128]{2,1,0:T(8,128)(2,1)S(1)} fusion(f32[4,8,256,128]{3,2,1,0:T(8,128)} %fusion.17, bf16[32,32,8,128]{3,2,1,0:T(8,128)(2,1)S(1)} %copy-done.11, f32[32,256,256]{1,2,0:T(8,128)} %get-tuple-element.69, f32[32,256]{1,0:T(8,128)S(1)} %get-tuple-element.68), kind=kOutput, calls=%fused_computation.17 | convolution fusion | flops 543162368 | bytes 16809984 | tf_op jit(solution)/shard_map/while/body/eval_jaxpr/hqp,hpd->hqd/dot_general | solution.py:167
  78.3 0.6 copy-done.16
  78.8 2.9 fusion.39
  81.7 4.7 fusion.20
  86.4 16.8 %fusion.9 = f32[32,256,128]{1,2,0:T(8,128)} fusion(f32[32,256,256]{1,2,0:T(8,128)} %fusion.20, bf16[32,256,32]{2,1,0:T(8,128)(2,1)} %get-tuple-element.51, bf16[32,256,32]{2,1,0:T(8,128)(2,1)} %get-tuple-element.50, bf16[32,256,64]{2,1,0:T(8,128)(2,1)} %get-tuple-element.54, f32[32,256,256]{1,2,0:T(8,128)} %get-tuple-element.69, ...), kind=kOutput, calls=%fused_computation.15 | convolution fusion | flops 557850880 | bytes 23101440 | tf_op jit(solution)/shard_map/while/body/eval_jaxpr/hqp,hqd->hpd/dot_general | solution.py:177
  103.2 2.5 slice_reduce_fusion
  105.7 1.7 slice.94
  107.5 3.7 fusion.83
  111.1 1.6 convolution_add_fusion
  112.7 0.0 all-reduce.9.cloned.1.call-update
  112.7 0.0 all-reduce.7.cloned.1.call-start
  112.8 2.8 fusion.84
  115.6 4.7 fusion.85
  120.3 25.4 %all-reduce.9.cloned.1.call-done = (f32[256,512]{1,0:T(8,128)}, f32[64,256]{1,0:T(8,128)}) async-done(((f32[256,512]{1,0:T(8,128)}, f32[64,256]{1,0:T(8,128)}), (f32[256,512]{1,0:T(8,128)}, f32[64,256]{1,0:T(8,128)})) %all-reduce.9.cloned.1.call-update) | async-done | bytes 589840 | tf_op jit(solution)/shard_map/psum | solution.py:200
  145.7 1.0 fusion.65
  146.6 1.2 multiply_reduce_fusion.1
  147.9 5.9 %convolution_bitcast_fusion = f32[4096,512]{0,1:T(8,128)} fusion(bf16[1,256,4096]{2,1,0:T(8,128)(2,1)S(1)} %copy-done, f32[256,512]{1,0:T(8,128)} %get-tuple-element.46, f32[256,512]{1,0:T(8,128)S(1)} %copy-done.6, f32[256]{0:T(256)S(1)} %broadcast_multiply_fusion, f32[256]{0:T(256)S(1)} %add_rsqrt_fusion), kind=kOutput, calls=%fused_computation.11 | convolution fusion | flops 1074397184 | bytes 11536384 | tf_op jit(solution)/shard_map/dot_general | solution.py:205
  153.8 1.5 fusion.29
  155.2 0.0 all-reduce.7.cloned.1.call-update
  155.2 379.9 %all-reduce.7.cloned.1.call-done = (f32[4096,512]{0,1:T(8,128)}, f32[64,4096]{1,0:T(8,128)}, f32[512,2048]{1,0:T(8,128)}, f32[512,4096]{1,0:T(8,128)}) async-done(((f32[4096,512]{0,1:T(8,128)}, f32[64,4096]{1,0:T(8,128)}, f32[512,2048]{1,0:T(8,128)}, f32[512,4096]{1,0:T(8,128)}), (f32[4096,512]{0,1:T(8,128)}, f32[64,4096]{1,0:T(8,128)}, f32[512,2048]{1,0:T(8,128)}, ...) | async-done | bytes 22020112 | tf_op jit(solution)/shard_map/psum | solution.py:207
  535.2 9.0 %copy.39 = f32[4096,512]{1,0:T(8,128)} copy(f32[4096,512]{0,1:T(8,128)} %get-tuple-element.42) | data formatting | bytes 16777216
  544.2 1.0 copy.69
  545.2 5.0 copy.70
  550.1 1.2 copy-done.7
  551.3 3.4 copy.71
  (33 shorter events, 0.1 us)
Async XLA Ops:
  7.2 1.6 copy-start
  7.2 41.4 %all-reduce.11.cloned.1.call-start = ((), (), s32[]{:S(2)}) async-start(), calls=%async_computation.2 | async-start | bytes 1179648 | tf_op jit(solution)/shard_map/psum | solution.py:112
  11.2 4.4 copy-start.15
  11.2 4.6 copy-start.13
  11.2 4.9 copy-start.14
  15.5 130.2 %all-reduce.9.cloned.1.call-start = ((), (), s32[]{:S(2)}) async-start(), calls=%async_computation.1 | async-start | bytes 1179648 | tf_op jit(solution)/shard_map/psum | solution.py:200
  27.2 1.6 copy-start.1
  58.5 5.4 copy-start.2
  58.5 5.4 copy-start.3
  58.5 5.4 copy-start.4
  58.5 5.4 copy-start.5
  67.3 4.6 copy-start.11
  71.9 7.0 %copy-start.16 = (f32[32,256,256]{1,2,0:T(8,128)S(1)}, f32[32,256,256]{1,2,0:T(8,128)}, u32[]{:S(2)}) copy-start(f32[32,256,256]{1,2,0:T(8,128)} %get-tuple-element.69) | copy-start | bytes 25165828
  103.2 4.3 copy-start.9
  107.4 3.7 copy-start.8
  112.7 422.4 %all-reduce.7.cloned.1.call-start = ((), (), s32[]{:S(2)}) async-start(), calls=%async_computation | async-start | bytes 44040192 | tf_op jit(solution)/shard_map/psum | solution.py:207
  112.8 2.8 copy-start.10
  115.6 31.1 %copy-start.6 = (f32[256,512]{1,0:T(8,128)S(1)}, f32[256,512]{1,0:T(8,128)}, u32[]{:S(2)}) copy-start(f32[256,512]{1,0:T(8,128)} %get-tuple-element.48) | copy-start | bytes 1572868
  535.2 9.0 %copy-start.12 = (f32[64,4096]{1,0:T(8,128)S(1)}, f32[64,4096]{1,0:T(8,128)}, u32[]{:S(2)}) copy-start(f32[64,4096]{1,0:T(8,128)} %get-tuple-element.71) | copy-start | bytes 3145732
  545.2 6.2 %copy-start.7 = (f32[512,4096]{1,0:T(8,128)S(1)}, f32[512,4096]{1,0:T(8,128)}, u32[]{:S(2)}) copy-start(f32[512,4096]{1,0:T(8,128)} %get-tuple-element.73) | copy-start | bytes 25165828
Sparse Core Ops, SparseCore 0:
  15.6 32.9 all-reduce.10
  112.9 32.7 all-reduce.8
  155.3 379.7 all-reduce.6
